TPU v7x, 128 devices: a whole 4x4x4 slice. The times are simulated.
128 devices in a mesh: rcv: 8 (over z_hi, y), src: 16 (over z_lo, x, core).
Axes of the slice: x: 4, y: 4, z: 4 (z_hi: 2, z_lo: 2; z = z_hi * 2 + z_lo), core: 2. Of those that a mesh axis runs over, the one named last changes fastest.
Arguments:
- kernel: bfloat16 [6912, 110592], P('rcv', 'src'), may hold values from -0.02734375 to 0.02734375
- rates: float32 [110592, 256], P(('rcv', 'src')), may hold values from 0.1 to 10
- state: float32 [6912, 256], P(('rcv', 'src')), may hold values from 0.1 to 10
- a_sigma: float32 [6912, 256], P(('rcv', 'src')), may hold values from 0.5 to 2
- b_sigma: float32 [6912, 256], P(('rcv', 'src')), may hold values from 0.5 to 2.5
- slip_distance: float32 [6912, 256], P(('rcv', 'src')), may hold values from 0.2 to 5
Outputs:
- rate_change: float32 [6912, 256], P(('rcv', 'src'))
- state_change: float32 [6912, 256], P(('rcv', 'src'))
All inputs are finite; a program needn't handle non-finite values.
Results may differ from a plain program's by a relative error of at most 0.0033.
Values may be sent and summed in bfloat16 or wider, within the bound.
A program may use at most 192 MiB of HBM per device.

v0:
```python
import jax
import jax.numpy as jnp
from jax import lax
from jax.sharding import PartitionSpec as P

damping = 0.5


def per_device(kernel, rates, state, a_sigma, b_sigma, slip_distance):
    deficit = (rates - 1.0).astype(jnp.bfloat16)
    patches = deficit.shape[0]
    rcv_count = lax.axis_size("rcv")
    src_count = lax.axis_size("src")
    column_size = patches * rcv_count
    src_place = lax.axis_index("src")
    rcv_place = lax.axis_index("rcv")
    rec_rows = state.shape[0]
    rec_block = rec_rows * src_count
    all_deficits = lax.all_gather(deficit, ("rcv", "src"), axis=0, tiled=True)
    sources = lax.dynamic_slice_in_dim(all_deficits, src_place * column_size, column_size, 0)
    own_deficit = lax.dynamic_slice_in_dim(
        all_deficits, rcv_place * rec_block + src_place * rec_rows, rec_rows, 0
    )
    partial_value = jnp.dot(kernel, sources, preferred_element_type=jnp.float32)
    stress = lax.psum_scatter(partial_value, "src", scatter_dimension=0, tiled=True)
    own_rate = own_deficit.astype(jnp.float32) + 1.0
    state_change = 1.0 - own_rate * state / slip_distance
    rate_change = (stress - b_sigma / state * state_change) / (a_sigma / own_rate + damping)
    return (rate_change, state_change)


def solution(mesh):
    in_specs = (
        P("rcv", "src"),
        P(("rcv", "src"), None),
        P(("rcv", "src"), None),
        P(("rcv", "src"), None),
        P(("rcv", "src"), None),
        P(("rcv", "src"), None),
    )
    out_specs = (P(("rcv", "src"), None), P(("rcv", "src"), None))
    return jax.shard_map(
        per_device, mesh=mesh, in_specs=in_specs, out_specs=out_specs, check_vma=False
    )
```

profile of v0, /device:TPU:24, one launch (start us, length us, event | category | flops | bytes accessed | tf_op | source)
XLA Modules:
  0.0 378.7 jit_solution(3102872758236283504)
XLA Ops:
  7.2 0.0 all-gather.2.cloned.1.call-start
  7.2 2.0 add_convert_fusion
  9.3 0.0 all-gather.2.cloned.1.call-update
  9.3 0.0 copy-start.4
  9.3 0.0 copy-start
  9.3 0.0 copy-start.1
  9.3 0.0 copy-start.2
  9.3 0.0 copy-start.3
  9.3 315.2 %all-gather.2.cloned.1.call-done = bf16[110592,256]{1,0:T(8,128)(2,1)} async-done(((bf16[864,256]{1,0:T(8,128)(2,1)}), bf16[110592,256]{1,0:T(8,128)(2,1)}) %all-gather.2.cloned.1.call-update) | async-done | bytes 56623120 | tf_op jit(solution)/shard_map/all_gather | solution.py:19
  324.6 7.2 %fusion.3 = f32[864,256]{1,0:T(8,128)S(1)} fusion(bf16[864,6912]{1,0:T(8,128)(2,1)} %param.6, bf16[110592,256]{1,0:T(8,128)(2,1)} %all-gather.2.cloned.1.call-done, s32[]{:T(128)S(6)} %select_n.6), kind=kOutput, calls=%fused_computation.2 | convolution fusion | flops 3057647616 | bytes 16367620 | tf_op jit(solution)/shard_map/dot_general | solution.py:24
  331.8 35.9 %fusion = f32[56,256]{1,0:T(8,128)S(1)} fusion(f32[864,256]{1,0:T(8,128)S(1)} %fusion.3), kind=kCustom, calls=%all-reduce-scatter | all-reduce-scatter fusion | flops 229377 | bytes 942592
  367.7 1.3 collective-permute-start
  369.0 0.0 copy-done.4
  369.0 0.6 dynamic-slice.4
  370.2 0.0 collective-permute-done
  370.2 0.2 concatenate
  370.4 0.0 copy-done
  370.4 0.0 copy-done.1
  370.4 0.0 copy-done.2
  370.4 0.0 copy-done.3
  370.4 1.5 fusion.6
  (1 shorter events, 0.0 us)
Async XLA Ops:
  7.2 317.4 %all-gather.2.cloned.1.call-start = ((), (), s32[]{:S(2)}) async-start(), calls=%async_computation | async-start | bytes 57065472 | tf_op jit(solution)/shard_map/all_gather | solution.py:19
  9.3 359.7 %copy-start.4 = (u32[128]{0:T(128)S(1)}, u32[128]{0:T(128)}, u32[]{:S(2)}) copy-start(u32[128]{0:T(128)} %constant.33) | copy-start | bytes 1540
  9.3 361.1 %copy-start = (f32[54,256]{1,0:T(8,128)S(1)}, f32[54,256]{1,0:T(8,128)}, u32[]{:S(2)}) copy-start(f32[54,256]{1,0:T(8,128)} %param.9) | copy-start | bytes 165892
  9.3 361.1 %copy-start.1 = (f32[54,256]{1,0:T(8,128)S(1)}, f32[54,256]{1,0:T(8,128)}, u32[]{:S(2)}) copy-start(f32[54,256]{1,0:T(8,128)} %param.10) | copy-start | bytes 165892
  9.3 361.1 %copy-start.2 = (f32[54,256]{1,0:T(8,128)S(1)}, f32[54,256]{1,0:T(8,128)}, u32[]{:S(2)}) copy-start(f32[54,256]{1,0:T(8,128)} %param.8) | copy-start | bytes 165892
  9.3 361.1 %copy-start.3 = (f32[54,256]{1,0:T(8,128)S(1)}, f32[54,256]{1,0:T(8,128)}, u32[]{:S(2)}) copy-start(f32[54,256]{1,0:T(8,128)} %param.11) | copy-start | bytes 165892
  367.7 2.6 collective-permute-start
Sparse Core Ops, SparseCore 0:
  9.7 314.7 all-gather.1
where the time goes:
time: 383 us; the launch traced here: 379 us
  waiting for transfers between devices  315 us (82%)
  blocking collectives  35.9 us (9%)
  between operations  14.8 us (4%)
  matrix products  7.2 us (2%)
    all_gather x1, waiting for transfers between devices, per_device(): all_deficits = lax.all_gather(deficit, ('rcv', 'src'), axis=0, tiled=True)  315 us
    unnamed x1, blocking collectives  35.9 us
  transfers between devices with their start and end apart: 2, of which 1 were waited for; matrix products, arithmetic and copies ran while one was open for 0% of the time, Pallas kernels for 0%

commit v1 on v0

v1 whole, which is shorter than its diff:
```python
import functools

import jax
import jax.numpy as jnp
from jax import lax
from jax.experimental import pallas as pl
from jax.experimental.pallas import tpu as pltpu
from jax.sharding import PartitionSpec as P

damping = 0.5
MESH = pl.DeviceIdType.MESH
LANES = 128


def gather_and_multiply(
    pr, qr, qc, kernel_ref, rates_ref, stress_ref, own_ref,
    kv, rv, pbuf, qbuf, dbuf, acc, sb, cb, rb, ob, od,
    k_sem, r_sem, pz_r, py_r, px_r, qy_r, d_r, rs_r, cx_r, od_r,
    pa_s, pb_s, py_s, px_s, qy_s, qx_s, qa_s, qb_s, cx_s, rs_s, od_s,
):
    r = lax.axis_index("rcv")
    s = lax.axis_index("src")
    y = lax.rem(r, 4)
    z = 2 * lax.div(r, 4) + lax.div(s, 8)
    x = lax.div(lax.rem(s, 8), 2)
    c = lax.rem(s, 2)
    zp = lax.rem(z, 2)
    p = 2 * x + c
    rows = pr + qr
    nq = qr // qc

    def m4(v):
        return lax.rem(v + 8, 4)

    def dev(dx, dy, dz, dc):
        return (4 * lax.div(dz, 2) + dy, 8 * lax.rem(dz, 2) + 2 * dx + dc)

    outer = (z == 0) | (z == 3)
    inner = jnp.logical_not(outer)
    home_core = c == zp
    owner = outer & home_core
    mid = inner & home_core
    relay = outer & jnp.logical_not(home_core)
    inner_i = jnp.where(inner, 1, 0)
    za = 3 * (1 - zp)
    zb = 1 + zp
    kk = jnp.where(z < 2, 1, 0)
    own_slot = jnp.where(outer, 2 * y + (1 - kk), 8)

    k_copy = pltpu.make_async_copy(kernel_ref, kv, k_sem)
    r_copy = pltpu.make_async_copy(rates_ref, rv, r_sem)
    r_copy.start()
    k_copy.start()

    bar = pltpu.get_barrier_semaphore()
    friends = [dev(x, m4(y + 1), z, c), dev(x, m4(y - 1), z, c), dev(x, y, m4(z + 1), c), dev(x, y, m4(z - 1), c)]
    friends += [dev(m4(x + d), y, z, 1 - c if k else c) for d in range(4) for k in range(2) if d or k]
    zx = z + 1 - 2 * zp
    friends += [dev(m4(x + d), y, zx, c) for d in range(1, 4)]
    for f in friends:
        pl.semaphore_signal(bar, inc=1, device_id=f, device_id_type=MESH)
    gives_own = (r == 0) & (s < 8)

    @pl.when(jnp.logical_not((r == 0) & (s == 0)))
    def _():
        pl.semaphore_signal(bar, inc=1, device_id=(0, r), device_id_type=MESH)

    r_copy.wait()
    for h in range(2):
        cols = slice(LANES * h, LANES * (h + 1))
        pbuf[h, own_slot] = (rv[:pr, cols] - 1.0).astype(jnp.bfloat16)
        qbuf[h, y] = (rv[pr:, cols] - 1.0).astype(jnp.bfloat16)

    pl.semaphore_wait(bar, len(friends) + jnp.where(gives_own, jnp.where(s == 0, 15, 16), 0))

    def remote(src, dst, ssem, rsem, to):
        return pltpu.make_async_remote_copy(
            src_ref=src, dst_ref=dst, send_sem=ssem, recv_sem=rsem, device_id=to, device_id_type=MESH
        )

    def landed(dst, sem):
        pltpu.make_async_copy(dst, dst, sem).wait()

    def qrows(piece, j):
        return pl.ds(pl.multiple_of(piece * rows + pr + j * qc, 16), qc)

    def prows(piece):
        return pl.ds(pl.multiple_of(piece * rows, 16), pr)

    def send_pa(h):
        dst = jnp.where(outer, 8, 2 * y + kk)
        sem = jnp.where(outer, 2, kk)
        remote(pbuf.at[h, own_slot], pbuf.at[h, dst], pa_s.at[h], pz_r.at[h, sem], dev(x, y, za, c)).start()

    def send_pb(h):
        remote(pbuf.at[h, 8], pbuf.at[h, 2 * y + kk], pb_s.at[h], pz_r.at[h, kk], dev(x, y, zb, c)).start()

    def send_py(h, e, k, way):
        slot = 2 * m4(y + e) + k
        to_e = (e - way) % 4 - 1
        remote(pbuf.at[h, slot], pbuf.at[h, slot], py_s.at[h], py_r.at[h, to_e, k], dev(x, m4(y + way), z, c)).start()

    def wait_py(h, e, k):
        landed(pbuf.at[h, 2 * m4(y + e) + k], py_r.at[h, (e % 4) - 1, k])

    def send_qy(h, e, j, way):
        part = qbuf.at[h, m4(y + e), pl.ds(j * qc, qc)]
        to_e = (e - way) % 4 - 1
        remote(part, part, qy_s.at[h], qy_r.at[h, to_e, j], dev(x, m4(y + way), z, c)).start()

    def wait_qy(h, e, j):
        landed(qbuf.at[h, m4(y + e), pl.ds(j * qc, qc)], qy_r.at[h, (e % 4) - 1, j])

    def send_px(h, e):
        to_x = m4(y + e)
        dst = dbuf.at[0, h, prows(p)]
        for k in range(2):
            core = 1 - c if k else c
            src = pbuf.at[h, 2 * to_x + core]
            there = remote(src, dst, px_s.at[h], px_r.at[h, p], dev(to_x, y, z, core))
            if k:
                there.start()
            else:
                pl.when(to_x != x)(there.start)
                here = pltpu.make_async_copy(src, dst, px_r.at[h, p])
                pl.when(to_x == x)(here.start)

    def send_qx(h, e, j):
        to_x = m4(y + e)
        src = qbuf.at[h, to_x, pl.ds(j * qc, qc)]
        dst = dbuf.at[inner_i, h, qrows(p, j)]
        sem = d_r.at[inner_i, h, p, j]
        me = (to_x == x) & home_core
        there = remote(src, dst, qx_s.at[h], sem, dev(to_x, y, z, zp))
        here = pltpu.make_async_copy(src, dst, sem)
        pl.when(jnp.logical_not(me))(there.start)
        pl.when(me)(here.start)

    def pass_z(h, piece, j):
        part = qrows(piece, j)
        final = dbuf.at[0, h, part]
        spare = dbuf.at[1, h, part]
        f_sem = d_r.at[0, h, piece, j]
        s_sem = d_r.at[1, h, piece, j]

        @pl.when(owner)
        def _():
            landed(final, f_sem)
            remote(final, spare, qa_s.at[h], s_sem, dev(x, y, za, c)).start()

        @pl.when(mid)
        def _():
            landed(spare, s_sem)
            remote(spare, final, qa_s.at[h], f_sem, dev(x, y, za, c)).start()
            remote(spare, final, qb_s.at[h], f_sem, dev(x, y, zb, c)).start()

        @pl.when(relay)
        def _():
            landed(spare, s_sem)
            remote(spare, final, qb_s.at[h], f_sem, dev(x, y, zb, c)).start()

    def start(h):
        send_pa(h)
        pl.when(inner)(functools.partial(send_pb, h))
        for j in range(nq):
            send_qy(h, 0, j, 1)
            send_qy(h, 0, j, -1)
        for j in range(nq):
            send_qx(h, 0, j)

    def q_ring(h):
        for j in range(nq):
            wait_qy(h, -1, j)
            if j % 2 == 0:
                send_qy(h, -1, j, 1)
            wait_qy(h, 1, j)
            if j % 2 == 1:
                send_qy(h, 1, j, -1)
            send_qx(h, -1, j)
            send_qx(h, 1, j)

    def q_far(h):
        for j in range(nq):
            wait_qy(h, 2, j)
            send_qx(h, 2, j)

    def p_relay(h):
        @pl.when(outer)
        def _():
            landed(pbuf.at[h, 8], pz_r.at[h, 2])
            send_pb(h)

    def p_slots(h):
        landed(pbuf.at[h, 2 * y + kk], pz_r.at[h, kk])

        @pl.when(inner)
        def _():
            landed(pbuf.at[h, 2 * y + 1 - kk], pz_r.at[h, 1 - kk])

        for k in range(2):
            send_py(h, 0, k, 1)
            send_py(h, 0, k, -1)
        send_px(h, 0)

    def p_ring(h):
        for k in range(2):
            wait_py(h, -1, k)
            if k == 0:
                send_py(h, -1, k, 1)
            wait_py(h, 1, k)
            if k == 1:
                send_py(h, 1, k, -1)
        send_px(h, -1)
        send_px(h, 1)

    def p_far(h):
        wait_py(h, 2, 0)
        wait_py(h, 2, 1)
        send_px(h, 2)

    def z_pass(h):
        for d in (0, 1, 3, 2):
            for cc in range(2):
                for j in range(nq):
                    pass_z(h, 2 * m4(x + d) + cc, j)

    depth = 768
    steps = kv.shape[1] // depth

    def product(h):
        for i in range(steps):
            if i < 8:
                landed(dbuf.at[0, h, prows(i)], px_r.at[h, i])

                @pl.when(jnp.logical_not(owner))
                def _():
                    for j in range(nq):
                        landed(dbuf.at[0, h, qrows(i, j)], d_r.at[0, h, i, j])

            part = jnp.dot(
                kv[:, i * depth:(i + 1) * depth], dbuf[0, h, i * depth:(i + 1) * depth],
                preferred_element_type=jnp.float32,
            )
            if i == 0:
                acc[...] = part
            else:
                acc[...] += part

    rec = rows // 16

    def sum_start(h):
        for b in range(16):
            sb[h, b % 2, b // 2, :rec] = acc[b * rec:(b + 1) * rec]
        remote(sb.at[h, 1 - c], cb.at[h], cx_s.at[h], cx_r.at[h], dev(x, y, z, 1 - c)).start()

    def sum_cores(h):
        landed(cb.at[h], cx_r.at[h])
        sb[h, c] = sb[h, c] + cb[h]
        for n in range(1, 8):
            to_x = m4(x + n % 4)
            to_z = zx if n >= 4 else z
            block = 4 * lax.rem(to_z, 2) + to_x
            remote(sb.at[h, c, block], rb.at[h, n], rs_s.at[h], rs_r.at[h, n], dev(to_x, y, to_z, c)).start()

    def sum_end(h):
        total = sb[h, c, 4 * zp + x]
        for n in range(1, 8):
            landed(rb.at[h, n], rs_r.at[h, n])
            total = total + rb[h, n]
        stress_ref[:, LANES * h:LANES * (h + 1)] = total[:rec]

    start(0)
    start(1)

    @pl.when(gives_own)
    def _():
        for b in range(16):
            ob[b, :rec] = (rv[b * rec:(b + 1) * rec] - 1.0).astype(jnp.bfloat16)
            there = remote(ob.at[b], od, od_s, od_r, (s, b))
            if b:
                there.start()
            else:
                pl.when(s != 0)(there.start)
                pl.when(s == 0)(pltpu.make_async_copy(ob.at[b], od, od_r).start)

    q_ring(0)
    p_relay(0)
    p_slots(0)
    q_far(0)
    q_ring(1)
    p_relay(1)
    p_ring(0)
    p_slots(1)
    z_pass(0)
    p_far(0)
    q_far(1)
    p_ring(1)
    p_far(1)
    k_copy.wait()
    z_pass(1)
    product(0)
    sum_start(0)
    sum_cores(0)
    product(1)
    sum_start(1)
    sum_cores(1)
    landed(od, od_r)
    own_ref[...] = od[:rec].astype(jnp.float32)
    sum_end(0)
    sum_end(1)

    def sent(sem, like, n=1):
        ref = like if n == 1 else like.at[pl.ds(0, n)]
        pltpu.make_async_copy(ref, ref, sem).wait()

    for h in range(2):
        sent(pa_s.at[h], pbuf.at[h, 0])
        sent(pb_s.at[h], pbuf.at[h, 0])
        sent(py_s.at[h], pbuf.at[h, pl.ds(0, 6)])
        sent(px_s.at[h], pbuf.at[h, pl.ds(0, 7)])
        sent(qy_s.at[h], qbuf.at[h, pl.ds(0, 3)])

        @pl.when(home_core)
        def _():
            sent(qx_s.at[h], qbuf.at[h, pl.ds(0, 3)])
            sent(qa_s.at[h], dbuf.at[0, h, pl.ds(0, 8 * qr)])

        @pl.when(jnp.logical_not(home_core))
        def _():
            sent(qx_s.at[h], qbuf.at[h, pl.ds(0, 4)])

        @pl.when(mid | relay)
        def _():
            sent(qb_s.at[h], dbuf.at[0, h, pl.ds(0, 8 * qr)])

        sent(cx_s.at[h], sb.at[h, 0])
        sent(rs_s.at[h], sb.at[h, 0, pl.ds(0, 7)])

    @pl.when(gives_own & (s != 0))
    def _():
        sent(od_s, ob)

    @pl.when(gives_own & (s == 0))
    def _():
        sent(od_s, ob.at[pl.ds(0, 15)])


def per_device(kernel, rates, state, a_sigma, b_sigma, slip_distance):
    patches, members = rates.shape
    rec_rows = state.shape[0]
    pr = 352
    qr = patches - pr
    qc = qr // 2
    nq = 2
    bf16, f32 = jnp.bfloat16, jnp.float32
    dma = pltpu.SemaphoreType.DMA
    rec_pad = -(-rec_rows // 8) * 8
    stress, own_deficit = pl.pallas_call(
        functools.partial(gather_and_multiply, pr, qr, qc),
        out_shape=[jax.ShapeDtypeStruct((rec_rows, members), f32)] * 2,
        in_specs=[pl.BlockSpec(memory_space=pl.ANY)] * 2,
        out_specs=[pl.BlockSpec(memory_space=pltpu.VMEM)] * 2,
        scratch_shapes=[
            pltpu.VMEM(kernel.shape, bf16),
            pltpu.VMEM(rates.shape, f32),
            pltpu.VMEM((2, 9, pr, LANES), bf16),
            pltpu.VMEM((2, 4, qr, LANES), bf16),
            pltpu.VMEM((2, 2, 8 * patches, LANES), bf16),
            pltpu.VMEM((patches, LANES), f32),
            pltpu.VMEM((2, 2, 8, rec_pad, LANES), f32),
            pltpu.VMEM((2, 8, rec_pad, LANES), f32),
            pltpu.VMEM((2, 8, rec_pad, LANES), f32),
            pltpu.VMEM((16, 64, members), bf16),
            pltpu.VMEM((64, members), bf16),
            dma, dma,
            dma((2, 3)), dma((2, 3, 2)), dma((2, 8)), dma((2, 3, nq)), dma((2, 2, 8, nq)),
            dma((2, 8)), dma((2,)), dma,
            dma((2,)), dma((2,)), dma((2,)), dma((2,)), dma((2,)), dma((2,)), dma((2,)), dma((2,)),
            dma((2,)), dma((2,)), dma,
        ],
        compiler_params=pltpu.CompilerParams(
            collective_id=0, has_side_effects=True, vmem_limit_bytes=48 * 2**20
        ),
        cost_estimate=pl.CostEstimate(
            flops=2 * kernel.size * members, bytes_accessed=kernel.size * 2 + rates.size * 4, transcendentals=0
        ),
    )(kernel, rates)
    own_rate = own_deficit + 1.0
    state_change = 1.0 - own_rate * state / slip_distance
    rate_change = (stress - b_sigma / state * state_change) / (a_sigma / own_rate + damping)
    return (rate_change, state_change)


def solution(mesh):
    rows = P(("rcv", "src"), None)
    return jax.shard_map(
        per_device, mesh=mesh, in_specs=(P("rcv", "src"), rows, rows, rows, rows, rows),
        out_specs=(rows, rows), check_vma=False,
    )
```

time: 383 us -> 80.7 us (0.21)
  the two profiles are of different devices: /device:TPU:24 before, /device:TPU:72 now
where the time goes in v1:
time: 80.7 us; the launch traced here: 80.6 us
  Pallas kernels  78 us (97%)
  local copies, waits for them, and re-layouts  1.18 us (1%)
    pallas_call x1, Pallas kernels, per_device(): pl.pallas_call(functools.partial(gather_and_multiply, pr, qr, qc), out_sh...  78 us

profile of v1, /device:TPU:72, one launch (start us, length us, event | category | flops | bytes accessed | tf_op | source)
XLA Modules:
  0.0 80.6 jit_solution(5098232513806439909)
XLA Ops:
  0.6 0.0 copy-start
  0.6 1.2 %copy-done = f32[864,256]{1,0:T(8,128)S(1)} copy-done((f32[864,256]{1,0:T(8,128)S(1)}, f32[864,256]{1,0:T(8,128)}, u32[]{:S(2)}) %copy-start) | copy-done | bytes 884760
  1.8 0.0 copy-start.1
  1.8 0.0 copy-start.2
  1.8 0.0 copy-start.3
  1.8 0.0 copy-start.4
  1.8 78.0 %shard_map.77 = (f32[54,256]{1,0:T(8,128)S(1)}, f32[54,256]{1,0:T(8,128)S(1)}) custom-call(bf16[864,6912]{1,0:T(8,128)(2,1)} %kernel_ref.1, f32[864,256]{1,0:T(8,128)S(1)} %copy-done), custom_call_target="tpu_custom_call" | custom-call | flops 3057647616 | bytes 12828672 | tf_op jit(solution)/shard_map/pallas_call | solution.py:358
  79.8 0.0 copy-done.1
  79.9 0.0 copy-done.2
  79.9 0.0 copy-done.3
  79.9 0.0 copy-done.4
  79.9 0.7 add_divide_fusion
Async XLA Ops:
  0.6 1.2 %copy-start = (f32[864,256]{1,0:T(8,128)S(1)}, f32[864,256]{1,0:T(8,128)}, u32[]{:S(2)}) copy-start(f32[864,256]{1,0:T(8,128)} %rates_ref.1) | copy-start | bytes 2654212
  1.8 78.0 %copy-start.1 = (f32[54,256]{1,0:T(8,128)S(1)}, f32[54,256]{1,0:T(8,128)}, u32[]{:S(2)}) copy-start(f32[54,256]{1,0:T(8,128)} %param.9) | copy-start | bytes 165892
  1.8 78.1 %copy-start.2 = (f32[54,256]{1,0:T(8,128)S(1)}, f32[54,256]{1,0:T(8,128)}, u32[]{:S(2)}) copy-start(f32[54,256]{1,0:T(8,128)} %param.10) | copy-start | bytes 165892
  1.8 78.1 %copy-start.3 = (f32[54,256]{1,0:T(8,128)S(1)}, f32[54,256]{1,0:T(8,128)}, u32[]{:S(2)}) copy-start(f32[54,256]{1,0:T(8,128)} %param.8) | copy-start | bytes 165892
  1.8 78.1 %copy-start.4 = (f32[54,256]{1,0:T(8,128)S(1)}, f32[54,256]{1,0:T(8,128)}, u32[]{:S(2)}) copy-start(f32[54,256]{1,0:T(8,128)} %param.11) | copy-start | bytes 165892

commit v2 on v0

v2 whole, which is shorter than its diff:
```python
import functools

import jax
import jax.numpy as jnp
from jax import lax
from jax.experimental import pallas as pl
from jax.experimental.pallas import tpu as pltpu
from jax.sharding import PartitionSpec as P

damping = 0.5
MESH = pl.DeviceIdType.MESH
LANES = 128
GROUPS = 3
CHUNKS = 2 * GROUPS


def gather_and_multiply(
    pc, qc, kernel_ref, rates_ref, stress_ref, own_ref,
    kv, kp, kq, rv, pbuf, qbuf, dp, dq, acc, sb, cb, rb, ob, od,
    k_sem, r_sem, pz_r, py_r, px_r, qy_r, d_r, rs_r, cx_r, od_r,
    pa_s, pb_s, py_s, px_s, qy_s, qx_s, qa_s, qb_s, cx_s, rs_s, od_s,
):
    r = lax.axis_index("rcv")
    s = lax.axis_index("src")
    y = lax.rem(r, 4)
    z = 2 * lax.div(r, 4) + lax.div(s, 8)
    x = lax.div(lax.rem(s, 8), 2)
    c = lax.rem(s, 2)
    zp = lax.rem(z, 2)
    p = 2 * x + c
    half = lax.div(x, 2)
    rows = GROUPS * (pc + qc)

    def m4(v):
        return lax.rem(v + 8, 4)

    def dev(dx, dy, dz, dc):
        return (4 * lax.div(dz, 2) + dy, 8 * lax.rem(dz, 2) + 2 * dx + dc)

    outer = (z == 0) | (z == 3)
    inner = jnp.logical_not(outer)
    home_core = c == zp
    owner = outer & home_core
    mid = inner & home_core
    relay = outer & jnp.logical_not(home_core)
    inner_i = jnp.where(inner, 1, 0)
    za = 3 * (1 - zp)
    zb = 1 + zp
    kk = jnp.where(z < 2, 1, 0)
    own_slot = jnp.where(outer, 2 * y + (1 - kk), 8)

    k_copy = pltpu.make_async_copy(kernel_ref, kv, k_sem)
    r_copy = pltpu.make_async_copy(rates_ref, rv, r_sem)
    r_copy.start()
    k_copy.start()

    bar = pltpu.get_barrier_semaphore()
    zx = z + 1 - 2 * zp
    friends = [dev(x, m4(y + 2), z, c)]
    friends += [dev(m4(x + d), y, zx, c) for d in (2, 1, 3)]
    friends += [dev(m4(x + d), y, z, 1 - c if k else c) for d in (2, 1, 3, 0) for k in range(2) if d or k]
    friends += [dev(x, m4(y + 1), z, c), dev(x, m4(y - 1), z, c), dev(x, y, m4(z + 1), c), dev(x, y, m4(z - 1), c)]
    gives_own = (r == 0) & (s < 8)

    @pl.when(jnp.logical_not((r == 0) & (s == 0)))
    def _():
        pl.semaphore_signal(bar, inc=1, device_id=(0, r), device_id_type=MESH)

    for f in friends:
        pl.semaphore_signal(bar, inc=1, device_id=f, device_id_type=MESH)

    r_copy.wait()

    def cols(t):
        return slice(LANES * (t // GROUPS), LANES * (t // GROUPS + 1))

    for t in range(CHUNKS):
        j = t % GROUPS
        qbuf[t, y] = (rv[GROUPS * pc + j * qc:GROUPS * pc + (j + 1) * qc, cols(t)] - 1.0).astype(jnp.bfloat16)
        pbuf[t, own_slot] = (rv[j * pc:(j + 1) * pc, cols(t)] - 1.0).astype(jnp.bfloat16)

    pl.semaphore_wait(bar, len(friends) + jnp.where(gives_own, jnp.where(s == 0, 15, 16), 0))

    def remote(src, dst, ssem, rsem, to):
        return pltpu.make_async_remote_copy(
            src_ref=src, dst_ref=dst, send_sem=ssem, recv_sem=rsem, device_id=to, device_id_type=MESH
        )

    def landed(dst, sem):
        pltpu.make_async_copy(dst, dst, sem).wait()

    def send_pa(t):
        dst = jnp.where(outer, 8, 2 * y + kk)
        sem = jnp.where(outer, 2, kk)
        remote(pbuf.at[t, own_slot], pbuf.at[t, dst], pa_s, pz_r.at[t, sem], dev(x, y, za, c)).start()

    def send_pb(t):
        remote(pbuf.at[t, 8], pbuf.at[t, 2 * y + kk], pb_s, pz_r.at[t, kk], dev(x, y, zb, c)).start()

    def p_relay(t):
        @pl.when(outer)
        def _():
            landed(pbuf.at[t, 8], pz_r.at[t, 2])
            send_pb(t)

    def p_slots(t):
        landed(pbuf.at[t, 2 * y + kk], pz_r.at[t, kk])

        @pl.when(inner)
        def _():
            landed(pbuf.at[t, 2 * y + 1 - kk], pz_r.at[t, 1 - kk])

        part = pbuf.at[t, pl.ds(2 * y, 2)]
        for d in (2, 1, 3):
            remote(part, part, py_s, py_r.at[t, d - 1], dev(x, m4(y + d), z, c)).start()

    def send_px(t, e):
        to_x = m4(y + e)
        dst = dp.at[t, p]
        for k in range(2):
            core = 1 - c if k else c
            src = pbuf.at[t, 2 * to_x + core]
            there = remote(src, dst, px_s, px_r.at[t], dev(to_x, y, z, core))
            if k:
                there.start()
            else:
                pl.when(to_x != x)(there.start)
                here = pltpu.make_async_copy(src, dst, px_r.at[t])
                pl.when(to_x == x)(here.start)

    def p_x(t):
        send_px(t, 0)
        for d in (1, 3, 2):
            landed(pbuf.at[t, pl.ds(2 * m4(y - d), 2)], py_r.at[t, d - 1])
            send_px(t, 4 - d)

    def send_qy(t):
        part = qbuf.at[t, y]
        for d in (2, 1, 3):
            remote(part, part, qy_s, qy_r.at[t, d - 1], dev(x, m4(y + d), z, c)).start()

    def send_qx(t, e):
        to_x = m4(y + e)
        src = qbuf.at[t, to_x]
        dst = dq.at[inner_i, t, p]
        sem = d_r.at[inner_i, t, half]
        me = (to_x == x) & home_core
        there = remote(src, dst, qx_s, sem, dev(to_x, y, z, zp))
        here = pltpu.make_async_copy(src, dst, sem)
        pl.when(jnp.logical_not(me))(there.start)
        pl.when(me)(here.start)

    def q_x(t):
        for d in (1, 3, 2):
            landed(qbuf.at[t, m4(y - d)], qy_r.at[t, d - 1])
            send_qx(t, 4 - d)

    def q_z(t):
        for g in range(2):
            final = dq.at[0, t, pl.ds(4 * g, 4)]
            spare = dq.at[1, t, pl.ds(4 * g, 4)]
            f_sem = d_r.at[0, t, g]
            s_sem = d_r.at[1, t, g]

            @pl.when(owner)
            def _():
                landed(final, f_sem)
                remote(final, spare, qa_s, s_sem, dev(x, y, za, c)).start()

            @pl.when(mid)
            def _():
                landed(spare, s_sem)
                remote(spare, final, qa_s, f_sem, dev(x, y, za, c)).start()
                remote(spare, final, qb_s, f_sem, dev(x, y, zb, c)).start()

    def q_relay(t):
        for g in range(2):
            final = dq.at[0, t, pl.ds(4 * g, 4)]
            spare = dq.at[1, t, pl.ds(4 * g, 4)]

            @pl.when(relay)
            def _():
                landed(spare, d_r.at[1, t, g])
                remote(spare, final, qb_s, d_r.at[0, t, g], dev(x, y, zb, c)).start()

    def regroup(j):
        @pl.loop(0, rows // 96)
        def _(i):
            at = pl.ds(pl.multiple_of(i * 96, 96), 96)
            for n in range(8):
                a = n * rows + j * pc
                kp[j, at, n * pc:(n + 1) * pc] = kv[at, a:a + pc]
                a = n * rows + GROUPS * pc + j * qc
                kq[j, at, n * qc:(n + 1) * qc] = kv[at, a:a + qc]

    def product(t):
        j = t % GROUPS
        landed(dp.at[t], px_r.at[t])
        part = jnp.dot(kp[j], dp[t].reshape(8 * pc, LANES), preferred_element_type=jnp.float32)
        if j == 0:
            acc[...] = part
        else:
            acc[...] += part

        @pl.when(jnp.logical_not(owner))
        def _():
            for g in range(2):
                landed(dq.at[0, t, pl.ds(4 * g, 4)], d_r.at[0, t, g])

        acc[...] += jnp.dot(kq[j], dq[0, t].reshape(8 * qc, LANES), preferred_element_type=jnp.float32)

    rec = rows // 16

    def sum_start(h):
        for b in range(16):
            sb[h, b % 2, b // 2, :rec] = acc[b * rec:(b + 1) * rec]
        remote(sb.at[h, 1 - c], cb.at[h], cx_s.at[h], cx_r.at[h], dev(x, y, z, 1 - c)).start()

    def sum_cores(h):
        landed(cb.at[h], cx_r.at[h])
        sb[h, c] = sb[h, c] + cb[h]
        for n in (6, 5, 7, 2, 1, 3, 4):
            to_x = m4(x + n % 4)
            to_z = zx if n >= 4 else z
            block = 4 * lax.rem(to_z, 2) + to_x
            remote(sb.at[h, c, block], rb.at[h, n], rs_s.at[h], rs_r.at[h, n], dev(to_x, y, to_z, c)).start()

    def sum_end(h):
        total = sb[h, c, 4 * zp + x]
        for n in range(1, 8):
            landed(rb.at[h, n], rs_r.at[h, n])
            total = total + rb[h, n]
        stress_ref[:, LANES * h:LANES * (h + 1)] = total[:rec]

    for t in range(CHUNKS):
        send_qy(t)
        send_pa(t)
        pl.when(inner)(functools.partial(send_pb, t))
    for t in range(CHUNKS):
        send_qx(t, 0)

    @pl.when(gives_own)
    def _():
        for b in range(16):
            ob[b, :rec] = (rv[b * rec:(b + 1) * rec] - 1.0).astype(jnp.bfloat16)
            there = remote(ob.at[b], od, od_s, od_r, (s, b))
            if b:
                there.start()
            else:
                pl.when(s != 0)(there.start)
                pl.when(s == 0)(pltpu.make_async_copy(ob.at[b], od, od_r).start)

    k_copy.wait()
    p_relay(0)
    p_relay(1)
    p_relay(2)
    q_x(0)
    p_relay(3)
    p_slots(0)
    p_relay(4)
    p_slots(1)
    q_x(1)
    p_relay(5)
    p_slots(2)
    p_slots(3)
    regroup(0)
    q_x(2)
    p_slots(4)
    q_z(0)
    p_slots(5)
    q_x(3)
    q_z(1)
    regroup(1)
    q_x(4)
    q_z(2)
    q_x(5)
    q_z(3)
    q_relay(0)
    regroup(2)
    q_z(4)
    p_x(0)
    q_z(5)
    q_relay(1)
    p_x(1)
    q_relay(2)
    p_x(2)
    product(0)
    q_relay(3)
    p_x(3)
    product(1)
    p_x(4)
    q_relay(4)
    product(2)
    sum_start(0)
    p_x(5)
    q_relay(5)
    sum_cores(0)
    product(3)
    product(4)
    sum_end(0)
    product(5)
    sum_start(1)
    sum_cores(1)
    landed(od, od_r)
    own_ref[...] = od[:rec].astype(jnp.float32)
    sum_end(1)

    def sent(sem, like):
        pltpu.make_async_copy(like, like, sem).wait()

    sent(pa_s, pbuf.at[:, 0])
    sent(pb_s, pbuf.at[:, 0])
    sent(py_s, pbuf.at[:, pl.ds(0, 6)])
    sent(px_s, pbuf.at[:, pl.ds(0, 7)])
    sent(qy_s, qbuf.at[:, pl.ds(0, 3)])

    @pl.when(home_core)
    def _():
        sent(qx_s, qbuf.at[:, pl.ds(0, 3)])
        sent(qa_s, dq.at[0])

    @pl.when(jnp.logical_not(home_core))
    def _():
        sent(qx_s, qbuf)

    @pl.when(mid | relay)
    def _():
        sent(qb_s, dq.at[0])

    for h in range(2):
        sent(cx_s.at[h], sb.at[h, 0])
        sent(rs_s.at[h], sb.at[h, 0, pl.ds(0, 7)])

    @pl.when(gives_own & (s != 0))
    def _():
        sent(od_s, ob)

    @pl.when(gives_own & (s == 0))
    def _():
        sent(od_s, ob.at[pl.ds(0, 15)])


def per_device(kernel, rates, state, a_sigma, b_sigma, slip_distance):
    patches, members = rates.shape
    rec_rows = state.shape[0]
    pc, qc = 128, 160
    bf16, f32 = jnp.bfloat16, jnp.float32
    dma = pltpu.SemaphoreType.DMA
    rec_pad = -(-rec_rows // 8) * 8
    stress, own_deficit = pl.pallas_call(
        functools.partial(gather_and_multiply, pc, qc),
        out_shape=[jax.ShapeDtypeStruct((rec_rows, members), f32)] * 2,
        in_specs=[pl.BlockSpec(memory_space=pl.ANY)] * 2,
        out_specs=[pl.BlockSpec(memory_space=pltpu.VMEM)] * 2,
        scratch_shapes=[
            pltpu.VMEM(kernel.shape, bf16),
            pltpu.VMEM((GROUPS, patches, 8 * pc), bf16),
            pltpu.VMEM((GROUPS, patches, 8 * qc), bf16),
            pltpu.VMEM(rates.shape, f32),
            pltpu.VMEM((CHUNKS, 9, pc, LANES), bf16),
            pltpu.VMEM((CHUNKS, 4, qc, LANES), bf16),
            pltpu.VMEM((CHUNKS, 8, pc, LANES), bf16),
            pltpu.VMEM((2, CHUNKS, 8, qc, LANES), bf16),
            pltpu.VMEM((patches, LANES), f32),
            pltpu.VMEM((2, 2, 8, rec_pad, LANES), f32),
            pltpu.VMEM((2, 8, rec_pad, LANES), f32),
            pltpu.VMEM((2, 8, rec_pad, LANES), f32),
            pltpu.VMEM((16, 64, members), bf16),
            pltpu.VMEM((64, members), bf16),
            dma, dma,
            dma((CHUNKS, 3)), dma((CHUNKS, 3)), dma((CHUNKS,)), dma((CHUNKS, 3)), dma((2, CHUNKS, 2)),
            dma((2, 8)), dma((2,)), dma,
            dma, dma, dma, dma, dma, dma, dma, dma, dma((2,)), dma((2,)), dma,
        ],
        compiler_params=pltpu.CompilerParams(
            collective_id=0, has_side_effects=True, vmem_limit_bytes=60 * 2**20
        ),
        cost_estimate=pl.CostEstimate(
            flops=2 * kernel.size * members, bytes_accessed=kernel.size * 2 + rates.size * 4, transcendentals=0
        ),
    )(kernel, rates)
    own_rate = own_deficit + 1.0
    state_change = 1.0 - own_rate * state / slip_distance
    rate_change = (stress - b_sigma / state * state_change) / (a_sigma / own_rate + damping)
    return (rate_change, state_change)


def solution(mesh):
    rows = P(("rcv", "src"), None)
    return jax.shard_map(
        per_device, mesh=mesh, in_specs=(P("rcv", "src"), rows, rows, rows, rows, rows),
        out_specs=(rows, rows), check_vma=False,
    )
```

time: 383 us -> 65.1 us (0.17); the launches traced: 379 us -> 65 us
  waiting for transfers between devices: 315 us -> 0 us
  Pallas kernels: 0 us -> 62.7 us
  blocking collectives: 35.9 us -> 0 us
  between operations: 14.8 us -> 0.7 us
  matrix products: 7.2 us -> 0 us
    all_gather x1 -> x0, waiting for transfers between devices: 315 us -> none  [per_device(): all_deficits = lax.all_gather(deficit, ('rcv', 'src'), axis=0, tiled=True)]
    pallas_call x0 -> x1, Pallas kernels: none -> 62.7 us  [per_device(): pl.pallas_call(functools.partial(gather_and_multiply, pc, qc), out_shape=...]
    unnamed x1 -> x0, blocking collectives: 35.9 us -> none
    dot_general x1 -> x0, matrix products: 7.2 us -> none  [per_device(): partial_value = jnp.dot(kernel, sources, preferred_element_type=jnp.float32)]
  transfers between devices with their start and end apart: 2 -> 0, of which waited for: 1 -> 0; matrix products, arithmetic and copies ran while one was open for 0% -> 0% of each run, Pallas kernels for 0% -> 0%
where the time goes in v2:
time: 65.1 us; the launch traced here: 65 us
  Pallas kernels  62.7 us (96%)
  other arithmetic  1.53 us (2%)
  between operations  0.7 us (1%)
    pallas_call x1, Pallas kernels, per_device(): pl.pallas_call(functools.partial(gather_and_multiply, pc, qc), out_shape=...  62.7 us
    div x1, other arithmetic, per_device(): (stress - b_sigma / state * state_change) / (a_sigma / own_rate + damping)  1.53 us

profile of v2, /device:TPU:24, one launch (start us, length us, event | category | flops | bytes accessed | tf_op | source)
XLA Modules:
  0.0 65.0 jit_solution(1233103041291407705)
XLA Ops:
  0.6 0.0 copy-start.3
  0.6 0.0 copy-start.1
  0.7 0.0 copy-start
  0.7 0.0 copy-start.2
  0.7 62.7 %shard_map.77 = (f32[54,256]{1,0:T(8,128)}, f32[54,256]{1,0:T(8,128)}) custom-call(bf16[864,6912]{1,0:T(8,128)(2,1)} %kernel_ref.1, f32[864,256]{1,0:T(8,128)} %rates_ref.1), custom_call_target="tpu_custom_call" | custom-call | flops 3057647616 | bytes 12828672 | tf_op jit(solution)/shard_map/pallas_call | solution.py:350
  63.4 0.0 copy-done.3
  63.4 0.0 copy-done.1
  63.4 0.0 copy-done
  63.4 0.0 copy-done.2
  63.4 1.5 %add_divide_fusion = (f32[54,256]{1,0:T(8,128)}, f32[54,256]{1,0:T(8,128)}) fusion(f32[54,256]{1,0:T(8,128)S(1)} %copy-done, f32[54,256]{1,0:T(8,128)} %get-tuple-element.4, f32[54,256]{1,0:T(8,128)S(1)} %copy-done.1, f32[54,256]{1,0:T(8,128)S(1)} %copy-done.2, f32[54,256]{1,0:T(8,128)} %get-tuple-element.5, f32[54,256]{1,0:T(8,128)S(1)} %copy-done.3), kind=kLoop, calls=%fused_computation | loop fusion | flops 138240 | bytes 442368 | tf_op jit(solution)/shard_map/div | solution.py:384
Async XLA Ops:
  0.6 62.8 %copy-start.3 = (f32[54,256]{1,0:T(8,128)S(1)}, f32[54,256]{1,0:T(8,128)}, u32[]{:S(2)}) copy-start(f32[54,256]{1,0:T(8,128)} %param.11) | copy-start | bytes 165892
  0.6 62.8 %copy-start.1 = (f32[54,256]{1,0:T(8,128)S(1)}, f32[54,256]{1,0:T(8,128)}, u32[]{:S(2)}) copy-start(f32[54,256]{1,0:T(8,128)} %param.10) | copy-start | bytes 165892
  0.7 62.8 %copy-start = (f32[54,256]{1,0:T(8,128)S(1)}, f32[54,256]{1,0:T(8,128)}, u32[]{:S(2)}) copy-start(f32[54,256]{1,0:T(8,128)} %param.9) | copy-start | bytes 165892
  0.7 62.8 %copy-start.2 = (f32[54,256]{1,0:T(8,128)S(1)}, f32[54,256]{1,0:T(8,128)}, u32[]{:S(2)}) copy-start(f32[54,256]{1,0:T(8,128)} %param.8) | copy-start | bytes 165892

commit v3 on v2

v3 whole, which is shorter than its diff:
```python
import functools

import jax
import jax.numpy as jnp
from jax import lax
from jax.experimental import pallas as pl
from jax.experimental.pallas import tpu as pltpu
from jax.sharding import PartitionSpec as P

damping = 0.5
MESH = pl.DeviceIdType.MESH
LANES = 128
P_GROUPS = (128, 128, 128)
Q_GROUPS = (160, 160, 160)
P_CHUNKS = ((0, 0), (0, 1), (0, 2), (1, 0), (1, 1), (1, 2))
Q_CHUNKS = ((0, 0), (0, 1), (0, 2), (1, 0), (1, 1), (1, 2))


def gather_and_multiply(
    kernel_ref, rates_ref, stress_ref, own_ref,
    kv, rv, pbuf, qbuf, acc, sb, cb, tb, rb, ob, od, op,
    k_sem, r_sem, pz_r, py_r, px_r, qy_r, d_r, rs_r, cx_r, od_r, op_r,
    pa_s, pb_s, py_s, px_s, qy_s, qx_s, qa_s, qb_s, cx_s, rs_s, od_s, op_s,
    *grouped,
):
    np_, nq_ = len(P_GROUPS), len(Q_GROUPS)
    kp, grouped = grouped[:np_], grouped[np_:]
    kq, grouped = grouped[:nq_], grouped[nq_:]
    dp, dq = grouped[:np_], grouped[np_:]
    p_rows = sum(P_GROUPS)
    p_at = [sum(P_GROUPS[:j]) for j in range(np_)]
    q_at = [sum(Q_GROUPS[:j]) for j in range(nq_)]
    r = lax.axis_index("rcv")
    s = lax.axis_index("src")
    y = lax.rem(r, 4)
    z = 2 * lax.div(r, 4) + lax.div(s, 8)
    x = lax.div(lax.rem(s, 8), 2)
    c = lax.rem(s, 2)
    zp = lax.rem(z, 2)
    p = 2 * x + c
    half = lax.div(x, 2)
    rows = p_rows + sum(Q_GROUPS)

    def m4(v):
        return lax.rem(v + 8, 4)

    def dev(dx, dy, dz, dc):
        return (4 * lax.div(dz, 2) + dy, 8 * lax.rem(dz, 2) + 2 * dx + dc)

    outer = (z == 0) | (z == 3)
    inner = jnp.logical_not(outer)
    home_core = c == zp
    owner = outer & home_core
    mid = inner & home_core
    relay = outer & jnp.logical_not(home_core)
    inner_i = jnp.where(inner, 1, 0)
    za = 3 * (1 - zp)
    zb = 1 + zp
    kk = jnp.where(z < 2, 1, 0)
    own_slot = jnp.where(outer, 2 * y + (1 - kk), 8)

    k_copy = pltpu.make_async_copy(kernel_ref, kv, k_sem)
    r_copy = pltpu.make_async_copy(rates_ref, rv, r_sem)
    r_copy.start()
    k_copy.start()

    bar = pltpu.get_barrier_semaphore()
    zx = z + 1 - 2 * zp
    friends = [dev(x, m4(y + 2), z, c)]
    friends += [dev(m4(x + d), y, zx, c) for d in (2, 1, 3)]
    friends += [dev(m4(x + d), y, z, 1 - c if k else c) for d in (2, 1, 3, 0) for k in range(2) if d or k]
    friends += [dev(x, m4(y + 1), z, c), dev(x, m4(y - 1), z, c), dev(x, y, m4(z + 1), c), dev(x, y, m4(z - 1), c)]
    gives_own = (s < 8) & (r == lax.rem(s, 4))
    in_own = s < 4

    @pl.when(jnp.logical_not((r < 4) & (s == r)))
    def _():
        pl.semaphore_signal(bar, inc=1, device_id=(lax.rem(r, 4), r), device_id_type=MESH)

    for f in friends:
        pl.semaphore_signal(bar, inc=1, device_id=f, device_id_type=MESH)

    r_copy.wait()

    for h in range(2):
        cols = slice(LANES * h, LANES * (h + 1))
        qbuf[h, y] = (rv[p_rows:, cols] - 1.0).astype(jnp.bfloat16)
        pbuf[h, own_slot] = (rv[:p_rows, cols] - 1.0).astype(jnp.bfloat16)

    pl.semaphore_wait(bar, len(friends) + jnp.where(gives_own, jnp.where(in_own, 15, 16), 0))

    def remote(src, dst, ssem, rsem, to):
        return pltpu.make_async_remote_copy(
            src_ref=src, dst_ref=dst, send_sem=ssem, recv_sem=rsem, device_id=to, device_id_type=MESH
        )

    def landed(dst, sem):
        pltpu.make_async_copy(dst, dst, sem).wait()

    def p_part(t, slot, n=None):
        h, j = P_CHUNKS[t]
        part = pl.ds(p_at[j], P_GROUPS[j])
        return pbuf.at[h, slot, part] if n is None else pbuf.at[h, pl.ds(slot, n), part]

    def q_part(t, slot):
        h, j = Q_CHUNKS[t]
        return qbuf.at[h, slot, pl.ds(q_at[j], Q_GROUPS[j])]

    def send_pa(t):
        dst = jnp.where(outer, 8, 2 * y + kk)
        sem = jnp.where(outer, 2, kk)
        remote(p_part(t, own_slot), p_part(t, dst), pa_s, pz_r.at[t, sem], dev(x, y, za, c)).start()

    def send_pb(t):
        remote(p_part(t, 8), p_part(t, 2 * y + kk), pb_s, pz_r.at[t, kk], dev(x, y, zb, c)).start()

    def p_relay(t):
        @pl.when(outer)
        def _():
            landed(p_part(t, 8), pz_r.at[t, 2])
            send_pb(t)

    def p_slots(t):
        landed(p_part(t, 2 * y + kk), pz_r.at[t, kk])

        @pl.when(inner)
        def _():
            landed(p_part(t, 2 * y + 1 - kk), pz_r.at[t, 1 - kk])

        part = p_part(t, 2 * y, 2)
        for d in (2, 1, 3):
            remote(part, part, py_s, py_r.at[t, d - 1], dev(x, m4(y + d), z, c)).start()

    def send_px(t, e):
        h, j = P_CHUNKS[t]
        to_x = m4(y + e)
        dst = dp[j].at[h, p]
        for k in range(2):
            core = 1 - c if k else c
            src = p_part(t, 2 * to_x + core)
            there = remote(src, dst, px_s, px_r.at[t], dev(to_x, y, z, core))
            if k:
                there.start()
            else:
                pl.when(to_x != x)(there.start)
                here = pltpu.make_async_copy(src, dst, px_r.at[t])
                pl.when(to_x == x)(here.start)

    def p_ring(t):
        send_px(t, 0)
        for d in (1, 3):
            landed(p_part(t, 2 * m4(y - d), 2), py_r.at[t, d - 1])
            send_px(t, 4 - d)

    def p_far(t):
        landed(p_part(t, 2 * m4(y + 2), 2), py_r.at[t, 1])
        send_px(t, 2)

    def send_qy(t):
        part = q_part(t, y)
        for d in (2, 1, 3):
            remote(part, part, qy_s, qy_r.at[t, d - 1], dev(x, m4(y + d), z, c)).start()

    def send_qx(t, e):
        h, j = Q_CHUNKS[t]
        to_x = m4(y + e)
        src = q_part(t, to_x)
        dst = dq[j].at[inner_i, h, p]
        sem = d_r.at[inner_i, t, half]
        me = (to_x == x) & home_core
        there = remote(src, dst, qx_s, sem, dev(to_x, y, z, zp))
        here = pltpu.make_async_copy(src, dst, sem)
        pl.when(jnp.logical_not(me))(there.start)
        pl.when(me)(here.start)

    def q_x(t):
        for d in (1, 3, 2):
            landed(q_part(t, m4(y - d)), qy_r.at[t, d - 1])
            send_qx(t, 4 - d)

    def q_ends(t, g):
        h, j = Q_CHUNKS[t]
        return [dq[j].at[n, h, pl.ds(4 * g, 4)] for n in range(2)] + [d_r.at[n, t, g] for n in range(2)]

    def q_z(t):
        for g in range(2):
            final, spare, f_sem, s_sem = q_ends(t, g)

            @pl.when(owner)
            def _():
                landed(final, f_sem)
                remote(final, spare, qa_s, s_sem, dev(x, y, za, c)).start()

            @pl.when(mid)
            def _():
                landed(spare, s_sem)
                remote(spare, final, qa_s, f_sem, dev(x, y, za, c)).start()
                remote(spare, final, qb_s, f_sem, dev(x, y, zb, c)).start()

    def q_relay(t):
        for g in range(2):
            final, spare, f_sem, s_sem = q_ends(t, g)

            @pl.when(relay)
            def _():
                landed(spare, s_sem)
                remote(spare, final, qb_s, f_sem, dev(x, y, zb, c)).start()

    def regroup(i):
        groups, at_, to, first = (P_GROUPS, p_at, kp, 0) if i < np_ else (Q_GROUPS, q_at, kq, p_rows)
        j = i if i < np_ else i - np_

        @pl.loop(0, rows // 96)
        def _(i):
            at = pl.ds(pl.multiple_of(i * 96, 96), 96)
            for n in range(8):
                a = n * rows + first + at_[j]
                to[j][at, n * groups[j]:(n + 1) * groups[j]] = kv[at, a:a + groups[j]]

    def add(first, k, d, n):
        part = jnp.dot(k[...], d.reshape(8 * n, LANES), preferred_element_type=jnp.float32)
        acc[...] = part if first else acc[...] + part

    started = []

    def p_mul(t):
        h, j = P_CHUNKS[t]
        landed(dp[j].at[h], px_r.at[t])
        add(h not in started, kp[j], dp[j][h], P_GROUPS[j])
        started.append(h)

    def q_mul(t):
        h, j = Q_CHUNKS[t]

        @pl.when(jnp.logical_not(owner))
        def _():
            for g in range(2):
                final, _, f_sem, _ = q_ends(t, g)
                landed(final, f_sem)

        add(h not in started, kq[j], dq[j][0, h], Q_GROUPS[j])
        started.append(h)

    rec = rows // 16

    def sum_start(h):
        for b in range(16):
            sb[h, b % 2, b // 2, :rec] = acc[b * rec:(b + 1) * rec]
        remote(sb.at[h, 1 - c], cb.at[h], cx_s.at[h], cx_r.at[h], dev(x, y, z, 1 - c)).start()

    def sum_cores(h):
        landed(cb.at[h], cx_r.at[h])
        tb[h, :, :rec] = (sb[h, c, :, :rec] + cb[h, :, :rec]).astype(jnp.bfloat16)
        for n in (6, 5, 7, 2, 1, 3, 4):
            to_x = m4(x + n % 4)
            to_z = zx if n >= 4 else z
            block = 4 * lax.rem(to_z, 2) + to_x
            remote(tb.at[h, block], rb.at[h, n], rs_s.at[h], rs_r.at[h, n], dev(to_x, y, to_z, c)).start()

    def sum_end(h):
        mine = 4 * zp + x
        total = sb[h, c, mine, :rec] + cb[h, mine, :rec]
        for n in range(1, 8):
            landed(rb.at[h, n], rs_r.at[h, n])
            total = total + rb[h, n, :rec].astype(jnp.float32)
        stress_ref[:, LANES * h:LANES * (h + 1)] = total

    keeps = (r == 0) & (lax.rem(s, 4) == 0)

    @pl.when((r == 0) & (s < 8))
    def _():
        part = pbuf.at[:, own_slot]

        @pl.when(keeps)
        def _():
            pltpu.make_async_copy(part, op, op_r).start()

        @pl.when(jnp.logical_not(keeps))
        def _():
            remote(part, op, op_s, op_r, (lax.rem(s, 4), s)).start()

    def own_pass():
        @pl.when(gives_own)
        def _():
            landed(op, op_r)
            for h in range(2):
                cols = slice(LANES * h, LANES * (h + 1))
                rv[:p_rows, cols] = op[h].astype(jnp.float32)
                rv[p_rows:, cols] = qbuf[h, 0].astype(jnp.float32)
            for b in range(16):
                ob[b, :rec] = rv[b * rec:(b + 1) * rec].astype(jnp.bfloat16)
                there = remote(ob.at[b], od, od_s, od_r, (s, b))
                if b < 4:
                    pl.when(s != b)(there.start)
                    pl.when(s == b)(pltpu.make_async_copy(ob.at[b], od, od_r).start)
                else:
                    there.start()

    for t in range(len(Q_CHUNKS)):
        send_qy(t)
    for t in range(len(P_CHUNKS)):
        send_pa(t)
        pl.when(inner)(functools.partial(send_pb, t))
    for t in range(len(Q_CHUNKS)):
        send_qx(t, 0)

    k_wait = k_copy.wait
    k_wait()
    p_relay(0)
    p_relay(1)
    p_relay(2)
    q_x(0)
    p_relay(3)
    p_slots(0)
    p_relay(4)
    p_slots(1)
    q_x(1)
    p_relay(5)
    p_slots(2)
    p_slots(3)
    regroup(0)
    regroup(1)
    q_x(2)
    p_slots(4)
    q_z(0)
    p_slots(5)
    q_x(3)
    q_z(1)
    regroup(2)
    regroup(3)
    q_x(4)
    q_z(2)
    q_x(5)
    q_z(3)
    own_pass()
    q_relay(0)
    regroup(4)
    regroup(5)
    q_z(4)
    p_ring(0)
    p_far(0)
    q_z(5)
    q_relay(1)
    p_ring(1)
    p_far(1)
    q_relay(2)
    p_ring(2)
    p_far(2)
    p_mul(0)
    q_mul(0)
    q_relay(3)
    p_ring(3)
    p_far(3)
    p_mul(1)
    q_mul(1)
    p_ring(4)
    p_far(4)
    q_relay(4)
    p_mul(2)
    q_mul(2)
    sum_start(0)
    p_ring(5)
    p_far(5)
    q_relay(5)
    sum_cores(0)
    p_mul(3)
    q_mul(3)
    p_mul(4)
    q_mul(4)
    p_mul(5)
    q_mul(5)
    sum_start(1)
    sum_end(0)
    sum_cores(1)
    landed(od, od_r)
    own_ref[...] = od[:rec].astype(jnp.float32)
    sum_end(1)

    def sent(sem, like):
        pltpu.make_async_copy(like, like, sem).wait()

    sent(pa_s, pbuf.at[:, 0])
    sent(pb_s, pbuf.at[:, 0])
    sent(py_s, pbuf.at[:, pl.ds(0, 6)])
    sent(px_s, pbuf.at[:, pl.ds(0, 7)])
    sent(qy_s, qbuf.at[:, pl.ds(0, 3)])

    @pl.when(home_core)
    def _():
        sent(qx_s, qbuf.at[:, pl.ds(0, 3)])

    @pl.when(jnp.logical_not(home_core))
    def _():
        sent(qx_s, qbuf)

    for j in range(nq_):
        @pl.when(home_core)
        def _():
            sent(qa_s, dq[j].at[0])

        @pl.when(mid | relay)
        def _():
            sent(qb_s, dq[j].at[0])

    for h in range(2):
        sent(cx_s.at[h], sb.at[h, 0])
        sent(rs_s.at[h], tb.at[h, pl.ds(0, 7)])

    @pl.when((r == 0) & (s < 8) & jnp.logical_not(keeps))
    def _():
        sent(op_s, op)

    @pl.when(gives_own & in_own)
    def _():
        sent(od_s, ob.at[pl.ds(0, 15)])

    @pl.when(gives_own & jnp.logical_not(in_own))
    def _():
        sent(od_s, ob)


def per_device(kernel, rates, state, a_sigma, b_sigma, slip_distance):
    patches, members = rates.shape
    rec_rows = state.shape[0]
    p_rows, q_rows = sum(P_GROUPS), sum(Q_GROUPS)
    assert p_rows + q_rows == patches
    p_chunks, q_chunks = len(P_CHUNKS), len(Q_CHUNKS)
    bf16, f32 = jnp.bfloat16, jnp.float32
    dma = pltpu.SemaphoreType.DMA
    rec_pad = -(-rec_rows // 8) * 8
    stress, own_deficit = pl.pallas_call(
        gather_and_multiply,
        out_shape=[jax.ShapeDtypeStruct((rec_rows, members), f32)] * 2,
        in_specs=[pl.BlockSpec(memory_space=pl.ANY)] * 2,
        out_specs=[pl.BlockSpec(memory_space=pltpu.VMEM)] * 2,
        scratch_shapes=[
            pltpu.VMEM(kernel.shape, bf16),
            pltpu.VMEM(rates.shape, f32),
            pltpu.VMEM((2, 9, p_rows, LANES), bf16),
            pltpu.VMEM((2, 4, q_rows, LANES), bf16),
            pltpu.VMEM((patches, LANES), f32),
            pltpu.VMEM((2, 2, 8, rec_pad, LANES), f32),
            pltpu.VMEM((2, 8, rec_pad, LANES), f32),
            pltpu.VMEM((2, 8, 64, LANES), bf16),
            pltpu.VMEM((2, 8, 64, LANES), bf16),
            pltpu.VMEM((16, 64, members), bf16),
            pltpu.VMEM((64, members), bf16),
            pltpu.VMEM((2, p_rows, LANES), bf16),
            dma, dma,
            dma((p_chunks, 3)), dma((p_chunks, 3)), dma((p_chunks,)),
            dma((q_chunks, 3)), dma((2, q_chunks, 2)),
            dma((2, 8)), dma((2,)), dma, dma,
            dma, dma, dma, dma, dma, dma, dma, dma, dma((2,)), dma((2,)), dma, dma,
            *[pltpu.VMEM((patches, 8 * n), bf16) for n in P_GROUPS],
            *[pltpu.VMEM((patches, 8 * n), bf16) for n in Q_GROUPS],
            *[pltpu.VMEM((2, 8, n, LANES), bf16) for n in P_GROUPS],
            *[pltpu.VMEM((2, 2, 8, n, LANES), bf16) for n in Q_GROUPS],
        ],
        compiler_params=pltpu.CompilerParams(
            collective_id=0, has_side_effects=True, vmem_limit_bytes=60 * 2**20
        ),
        cost_estimate=pl.CostEstimate(
            flops=2 * kernel.size * members, bytes_accessed=kernel.size * 2 + rates.size * 4, transcendentals=0
        ),
    )(kernel, rates)
    own_rate = own_deficit + 1.0
    state_change = 1.0 - own_rate * state / slip_distance
    rate_change = (stress - b_sigma / state * state_change) / (a_sigma / own_rate + damping)
    return (rate_change, state_change)


def solution(mesh):
    rows = P(("rcv", "src"), None)
    return jax.shard_map(
        per_device, mesh=mesh, in_specs=(P("rcv", "src"), rows, rows, rows, rows, rows),
        out_specs=(rows, rows), check_vma=False,
    )
```

time: 65.1 us -> 59.4 us (0.912)
  Pallas kernels: 62.7 us -> 56.5 us
    pallas_call x1, Pallas kernels: 62.7 us -> 56.5 us  [per_device(): pl.pallas_call(gather_and_multiply, out_shape=[jax.ShapeDtypeStruct((rec_...]
where the time goes in v3:
time: 59.4 us; the launch traced here: 58.8 us
  Pallas kernels  56.5 us (95%)
  other arithmetic  1.53 us (3%)
  between operations  0.7 us (1%)
    pallas_call x1, Pallas kernels, per_device(): pl.pallas_call(gather_and_multiply, out_shape=[jax.ShapeDtypeStruct((rec_...  56.5 us
    div x1, other arithmetic, per_device(): (stress - b_sigma / state * state_change) / (a_sigma / own_rate + damping)  1.53 us

profile of v3, /device:TPU:24, one launch (start us, length us, event | category | flops | bytes accessed | tf_op | source)
XLA Modules:
  0.0 58.8 jit_solution(9346916329064123303)
XLA Ops:
  0.6 0.0 copy-start.3
  0.6 0.0 copy-start.1
  0.7 0.0 copy-start
  0.7 0.0 copy-start.2
  0.7 56.5 %shard_map.77 = (f32[54,256]{1,0:T(8,128)}, f32[54,256]{1,0:T(8,128)}) custom-call(bf16[864,6912]{1,0:T(8,128)(2,1)} %kernel_ref.1, f32[864,256]{1,0:T(8,128)} %rates_ref.1), custom_call_target="tpu_custom_call" | custom-call | flops 3057647616 | bytes 12828672 | tf_op jit(solution)/shard_map/pallas_call | solution.py:431
  57.2 0.0 copy-done.3
  57.2 0.0 copy-done.1
  57.2 0.0 copy-done
  57.2 0.0 copy-done.2
  57.2 1.5 %add_divide_fusion = (f32[54,256]{1,0:T(8,128)}, f32[54,256]{1,0:T(8,128)}) fusion(f32[54,256]{1,0:T(8,128)S(1)} %copy-done, f32[54,256]{1,0:T(8,128)} %get-tuple-element.4, f32[54,256]{1,0:T(8,128)S(1)} %copy-done.1, f32[54,256]{1,0:T(8,128)S(1)} %copy-done.2, f32[54,256]{1,0:T(8,128)} %get-tuple-element.5, f32[54,256]{1,0:T(8,128)S(1)} %copy-done.3), kind=kLoop, calls=%fused_computation | loop fusion | flops 138240 | bytes 442368 | tf_op jit(solution)/shard_map/div | solution.py:468
Async XLA Ops:
  0.6 56.5 %copy-start.3 = (f32[54,256]{1,0:T(8,128)S(1)}, f32[54,256]{1,0:T(8,128)}, u32[]{:S(2)}) copy-start(f32[54,256]{1,0:T(8,128)} %param.11) | copy-start | bytes 165892
  0.6 56.5 %copy-start.1 = (f32[54,256]{1,0:T(8,128)S(1)}, f32[54,256]{1,0:T(8,128)}, u32[]{:S(2)}) copy-start(f32[54,256]{1,0:T(8,128)} %param.10) | copy-start | bytes 165892
  0.7 56.5 %copy-start = (f32[54,256]{1,0:T(8,128)S(1)}, f32[54,256]{1,0:T(8,128)}, u32[]{:S(2)}) copy-start(f32[54,256]{1,0:T(8,128)} %param.9) | copy-start | bytes 165892
  0.7 56.5 %copy-start.2 = (f32[54,256]{1,0:T(8,128)S(1)}, f32[54,256]{1,0:T(8,128)}, u32[]{:S(2)}) copy-start(f32[54,256]{1,0:T(8,128)} %param.8) | copy-start | bytes 165892

commit v4 on v3

--- a/solution.py
+++ b/solution.py
@@ -10,10 +10,10 @@
 damping = 0.5
 MESH = pl.DeviceIdType.MESH
 LANES = 128
-P_GROUPS = (128, 128, 128)
-Q_GROUPS = (160, 160, 160)
-P_CHUNKS = ((0, 0), (0, 1), (0, 2), (1, 0), (1, 1), (1, 2))
-Q_CHUNKS = ((0, 0), (0, 1), (0, 2), (1, 0), (1, 1), (1, 2))
+P_GROUPS = (96, 144, 144)
+Q_GROUPS = (128, 176, 176)
+P_CHUNKS = ((0, 0), (0, 1), (0, 2), (1, 1), (1, 2), (1, 0))
+Q_CHUNKS = ((0, 0), (0, 1), (0, 2), (1, 1), (1, 2), (1, 0))
 
 
 def gather_and_multiply(
@@ -128,7 +128,7 @@
             landed(p_part(t, 2 * y + 1 - kk), pz_r.at[t, 1 - kk])
 
         part = p_part(t, 2 * y, 2)
-        for d in (2, 1, 3):
+        for d in (1, 3, 2):
             remote(part, part, py_s, py_r.at[t, d - 1], dev(x, m4(y + d), z, c)).start()
 
     def send_px(t, e):
@@ -337,18 +337,18 @@
     regroup(4)
     regroup(5)
     q_z(4)
+    q_relay(1)
     p_ring(0)
     p_far(0)
     q_z(5)
-    q_relay(1)
     p_ring(1)
     p_far(1)
     q_relay(2)
     p_ring(2)
     p_far(2)
-    p_mul(0)
     q_mul(0)
     q_relay(3)
+    p_mul(0)
     p_ring(3)
     p_far(3)
     p_mul(1)

time: 59.4 us -> 58 us (0.976)
  Pallas kernels: 56.5 us -> 55.5 us
    pallas_call x1, Pallas kernels: 56.5 us -> 55.5 us  [per_device(): pl.pallas_call(gather_and_multiply, out_shape=[jax.ShapeDtypeStruct((rec_...]
where the time goes in v4:
time: 58 us; the launch traced here: 57.7 us
  Pallas kernels  55.5 us (96%)
  other arithmetic  1.53 us (3%)
  between operations  0.7 us (1%)
    pallas_call x1, Pallas kernels, per_device(): pl.pallas_call(gather_and_multiply, out_shape=[jax.ShapeDtypeStruct((rec_...  55.5 us
    div x1, other arithmetic, per_device(): (stress - b_sigma / state * state_change) / (a_sigma / own_rate + damping)  1.53 us

profile of v4, /device:TPU:24, one launch (start us, length us, event | category | flops | bytes accessed | tf_op | source)
XLA Modules:
  0.0 57.7 jit_solution(17575818726149766245)
XLA Ops:
  0.6 0.0 copy-start.3
  0.6 0.0 copy-start.1
  0.7 0.0 copy-start
  0.7 0.0 copy-start.2
  0.7 55.5 %shard_map.77 = (f32[54,256]{1,0:T(8,128)}, f32[54,256]{1,0:T(8,128)}) custom-call(bf16[864,6912]{1,0:T(8,128)(2,1)} %kernel_ref.1, f32[864,256]{1,0:T(8,128)} %rates_ref.1), custom_call_target="tpu_custom_call" | custom-call | flops 3057647616 | bytes 12828672 | tf_op jit(solution)/shard_map/pallas_call | solution.py:431
  56.2 0.0 copy-done.3
  56.2 0.0 copy-done.1
  56.2 0.0 copy-done
  56.2 0.0 copy-done.2
  56.2 1.5 %add_divide_fusion = (f32[54,256]{1,0:T(8,128)}, f32[54,256]{1,0:T(8,128)}) fusion(f32[54,256]{1,0:T(8,128)S(1)} %copy-done, f32[54,256]{1,0:T(8,128)} %get-tuple-element.4, f32[54,256]{1,0:T(8,128)S(1)} %copy-done.1, f32[54,256]{1,0:T(8,128)S(1)} %copy-done.2, f32[54,256]{1,0:T(8,128)} %get-tuple-element.5, f32[54,256]{1,0:T(8,128)S(1)} %copy-done.3), kind=kLoop, calls=%fused_computation | loop fusion | flops 138240 | bytes 442368 | tf_op jit(solution)/shard_map/div | solution.py:468
Async XLA Ops:
  0.6 55.5 %copy-start.3 = (f32[54,256]{1,0:T(8,128)S(1)}, f32[54,256]{1,0:T(8,128)}, u32[]{:S(2)}) copy-start(f32[54,256]{1,0:T(8,128)} %param.11) | copy-start | bytes 165892
  0.6 55.5 %copy-start.1 = (f32[54,256]{1,0:T(8,128)S(1)}, f32[54,256]{1,0:T(8,128)}, u32[]{:S(2)}) copy-start(f32[54,256]{1,0:T(8,128)} %param.10) | copy-start | bytes 165892
  0.7 55.5 %copy-start = (f32[54,256]{1,0:T(8,128)S(1)}, f32[54,256]{1,0:T(8,128)}, u32[]{:S(2)}) copy-start(f32[54,256]{1,0:T(8,128)} %param.9) | copy-start | bytes 165892
  0.7 55.5 %copy-start.2 = (f32[54,256]{1,0:T(8,128)S(1)}, f32[54,256]{1,0:T(8,128)}, u32[]{:S(2)}) copy-start(f32[54,256]{1,0:T(8,128)} %param.8) | copy-start | bytes 165892

commit v5 on v4

--- a/solution.py
+++ b/solution.py
@@ -256,6 +256,47 @@
             to_z = zx if n >= 4 else z
             block = 4 * lax.rem(to_z, 2) + to_x
             remote(tb.at[h, block], rb.at[h, n], rs_s.at[h], rs_r.at[h, n], dev(to_x, y, to_z, c)).start()
+
+    part_rows = rows // 2
+
+    def parts():
+        return [(0, 1 - zp, (6, 5, 7, 4)), (1, zp, (2, 1, 3))]
+
+    def finish_first():
+        t, u = len(P_CHUNKS) - 1, len(Q_CHUNKS) - 1
+        h, j = P_CHUNKS[t]
+        _, i = Q_CHUNKS[u]
+        landed(dp[j].at[h], px_r.at[t])
+
+        @pl.when(jnp.logical_not(owner))
+        def _():
+            for g in range(2):
+                final, _, f_sem, _ = q_ends(u, g)
+                landed(final, f_sem)
+
+        p_vals = dp[j][h].reshape(8 * P_GROUPS[j], LANES)
+        q_vals = dq[i][0, h].reshape(8 * Q_GROUPS[i], LANES)
+        for g, lo, _ in parts():
+            at = pl.ds(pl.multiple_of(lo * part_rows, 16), part_rows)
+            part = acc[at]
+            part += jnp.dot(kp[j][at], p_vals, preferred_element_type=jnp.float32)
+            part += jnp.dot(kq[i][at], q_vals, preferred_element_type=jnp.float32)
+            for b in range(8):
+                sb[h, b % 2, 4 * lo + b // 2, :rec] = part[b * rec:(b + 1) * rec]
+            four = pl.ds(4 * lo, 4)
+            remote(sb.at[h, 1 - c, four], cb.at[h, four], cx_s.at[h], cx_r.at[1 + g], dev(x, y, z, 1 - c)).start()
+
+    def finish_last():
+        h = 1
+        for g, lo, targets in parts():
+            four = pl.ds(4 * lo, 4)
+            landed(cb.at[h, four], cx_r.at[1 + g])
+            tb[h, four, :rec] = (sb[h, c, four, :rec] + cb[h, four, :rec]).astype(jnp.bfloat16)
+            for n in targets:
+                to_x = m4(x + n % 4)
+                block = 4 * lo + to_x
+                to = dev(to_x, y, zx if n >= 4 else z, c)
+                remote(tb.at[h, block], rb.at[h, n], rs_s.at[h], rs_r.at[h, n], to).start()
 
     def sum_end(h):
         mine = 4 * zp + x
@@ -367,11 +408,9 @@
     q_mul(3)
     p_mul(4)
     q_mul(4)
-    p_mul(5)
-    q_mul(5)
-    sum_start(1)
+    finish_first()
     sum_end(0)
-    sum_cores(1)
+    finish_last()
     landed(od, od_r)
     own_ref[...] = od[:rec].astype(jnp.float32)
     sum_end(1)
@@ -449,7 +488,7 @@
             dma, dma,
             dma((p_chunks, 3)), dma((p_chunks, 3)), dma((p_chunks,)),
             dma((q_chunks, 3)), dma((2, q_chunks, 2)),
-            dma((2, 8)), dma((2,)), dma, dma,
+            dma((2, 8)), dma((3,)), dma, dma,
             dma, dma, dma, dma, dma, dma, dma, dma, dma((2,)), dma((2,)), dma, dma,
             *[pltpu.VMEM((patches, 8 * n), bf16) for n in P_GROUPS],
             *[pltpu.VMEM((patches, 8 * n), bf16) for n in Q_GROUPS],

time: 58 us -> 57.7 us (level)
  Pallas kernels: 55.5 us -> 54.7 us
    pallas_call x1, Pallas kernels: 55.5 us -> 54.7 us  [per_device(): pl.pallas_call(gather_and_multiply, out_shape=[jax.ShapeDtypeStruct((rec_...]
where the time goes in v5:
time: 57.7 us; the launch traced here: 56.9 us
  Pallas kernels  54.7 us (95%)
  other arithmetic  1.53 us (3%)
  between operations  0.7 us (1%)
    pallas_call x1, Pallas kernels, per_device(): pl.pallas_call(gather_and_multiply, out_shape=[jax.ShapeDtypeStruct((rec_...  54.7 us
    div x1, other arithmetic, per_device(): (stress - b_sigma / state * state_change) / (a_sigma / own_rate + damping)  1.53 us

profile of v5, /device:TPU:24, one launch (start us, length us, event | category | flops | bytes accessed | tf_op | source)
XLA Modules:
  0.0 56.9 jit_solution(13675963997567955862)
XLA Ops:
  0.6 0.0 copy-start.3
  0.6 0.0 copy-start.1
  0.7 0.0 copy-start
  0.7 0.0 copy-start.2
  0.7 54.7 %shard_map.77 = (f32[54,256]{1,0:T(8,128)}, f32[54,256]{1,0:T(8,128)}) custom-call(bf16[864,6912]{1,0:T(8,128)(2,1)} %kernel_ref.1, f32[864,256]{1,0:T(8,128)} %rates_ref.1), custom_call_target="tpu_custom_call" | custom-call | flops 3057647616 | bytes 12828672 | tf_op jit(solution)/shard_map/pallas_call | solution.py:470
  55.4 0.0 copy-done.3
  55.4 0.0 copy-done.1
  55.4 0.0 copy-done
  55.4 0.0 copy-done.2
  55.4 1.5 %add_divide_fusion = (f32[54,256]{1,0:T(8,128)}, f32[54,256]{1,0:T(8,128)}) fusion(f32[54,256]{1,0:T(8,128)S(1)} %copy-done, f32[54,256]{1,0:T(8,128)} %get-tuple-element.4, f32[54,256]{1,0:T(8,128)S(1)} %copy-done.1, f32[54,256]{1,0:T(8,128)S(1)} %copy-done.2, f32[54,256]{1,0:T(8,128)} %get-tuple-element.5, f32[54,256]{1,0:T(8,128)S(1)} %copy-done.3), kind=kLoop, calls=%fused_computation | loop fusion | flops 138240 | bytes 442368 | tf_op jit(solution)/shard_map/div | solution.py:507
Async XLA Ops:
  0.6 54.7 %copy-start.3 = (f32[54,256]{1,0:T(8,128)S(1)}, f32[54,256]{1,0:T(8,128)}, u32[]{:S(2)}) copy-start(f32[54,256]{1,0:T(8,128)} %param.11) | copy-start | bytes 165892
  0.6 54.7 %copy-start.1 = (f32[54,256]{1,0:T(8,128)S(1)}, f32[54,256]{1,0:T(8,128)}, u32[]{:S(2)}) copy-start(f32[54,256]{1,0:T(8,128)} %param.10) | copy-start | bytes 165892
  0.7 54.7 %copy-start = (f32[54,256]{1,0:T(8,128)S(1)}, f32[54,256]{1,0:T(8,128)}, u32[]{:S(2)}) copy-start(f32[54,256]{1,0:T(8,128)} %param.9) | copy-start | bytes 165892
  0.7 54.7 %copy-start.2 = (f32[54,256]{1,0:T(8,128)S(1)}, f32[54,256]{1,0:T(8,128)}, u32[]{:S(2)}) copy-start(f32[54,256]{1,0:T(8,128)} %param.8) | copy-start | bytes 165892
